TPU v7x, 32 devices: a whole 2x2x4 slice. The times are simulated.
32 devices in a mesh: section: 2 (over y), expert: 8 (over z, core), dp: 2 (over x).
Axes of the slice: x: 2, y: 2, z: 4, core: 2. Of those that a mesh axis runs over, the one named last changes fastest.
Arguments:
- blocks: bfloat16 [2, 128, 7168], P('section', ('expert', 'dp')), may hold values from -6 to 6
- gains: float32 [2, 7168], P('section'), may hold values from 0.1 to 1.9
- w_gate: bfloat16 [2, 7168, 2048], P('section', 'dp', 'expert'), may hold values from -0.0625 to 0.0625
- w_up: bfloat16 [2, 7168, 2048], P('section', 'dp', 'expert'), may hold values from -0.0625 to 0.0625
- w_down: bfloat16 [2, 7168, 2048], P('section', 'dp', 'expert'), may hold values from -0.1875 to 0.1875
- expert_ids: int32 [2, 2, 128, 2], P('section', None, ('expert', 'dp')), may hold values from 0 to 1, all different within a row; in each aligned block of 8 rows (0 to 7, 8 to 15, ..., all dimensions but the last counted through in order) at most 8 rows name the same one
- combine: float32 [2, 2, 128, 2], P('section', None, ('expert', 'dp')), may hold values from 0.2 to 1
Outputs:
- finished: bfloat16 [2, 128, 7168], P('section', ('expert', 'dp'))
Inputs may be any that keep to these rules, and one draw needn't show every extreme that they name: `expert_ids`: each token names 2 different experts; within the 8 tokens of one device (aligned blocks), no expert is named more than 8 times, a bound that some block reaches.
All inputs are finite; a program needn't handle non-finite values.
Results may differ from a plain program's by a relative error of at most 0.0073.
Values may be sent and summed in bfloat16 or wider, within the bound.
A program may use at most 64 MiB of HBM per device.

v0:
```python
from functools import partial

import jax
import jax.numpy as jnp
from jax import lax
from jax.sharding import PartitionSpec as P


def passed_along(array, axis, by):
    length = lax.axis_size(axis)
    return lax.ppermute(array, axis, [(i, (i + by) % length) for i in range(length)])


def expert_rows(arrived, gate_full, up_full, down_full):
    sources, slot_count, model_width = arrived.shape
    flat_rows = arrived.reshape(sources * slot_count, model_width)
    gate_act = jnp.dot(flat_rows, gate_full, preferred_element_type=jnp.float32)
    upward = jnp.dot(flat_rows, up_full, preferred_element_type=jnp.float32)
    hidden = (jax.nn.silu(gate_act) * upward).astype(jnp.bfloat16)
    output = lax.dot_general(
        hidden, down_full, (((1,), (1,)), ((), ())), preferred_element_type=jnp.float32
    )
    output = output.astype(jnp.bfloat16).reshape(sources, slot_count, model_width)
    return lax.all_to_all(output, "expert", split_axis=0, concat_axis=0, tiled=True)


def moe_layer(stream, gain_row, weights, routes, mixing):
    owners = lax.axis_size("expert")
    experts = max(2, owners // 8)
    span = owners // experts
    tok_rows, model_width = stream.shape
    fan_out = routes.shape[1]
    capacity = min(tok_rows, max(2, 5 * tok_rows * fan_out // (4 * experts)))
    widened = stream.astype(jnp.float32)
    inv_rms = lax.rsqrt(jnp.mean(widened * widened, axis=1, keepdims=True) + 1e-06)
    normed = (widened * inv_rms * gain_row[None, :]).astype(jnp.bfloat16)
    flat_ids = routes.reshape(-1)
    count_all = flat_ids.shape[0]
    chosen = (flat_ids[:, None] == jnp.arange(experts, dtype=jnp.int32)[None, :]).astype(
        jnp.float32
    )
    triangle = (jnp.arange(count_all)[:, None] >= jnp.arange(count_all)[None, :]).astype(
        jnp.float32
    )
    running = jnp.dot(triangle, chosen, preferred_element_type=jnp.float32)
    slot_of = jnp.sum(chosen * (running - 1.0), axis=1).astype(jnp.int32)
    target = flat_ids * capacity + slot_of
    placing = jnp.arange(experts * capacity, dtype=jnp.int32)[:, None] == target[None, :]
    placing = (
        placing.reshape(experts * capacity, tok_rows, fan_out).any(axis=2).astype(jnp.bfloat16)
    )
    outgoing = jnp.dot(placing, normed, preferred_element_type=jnp.float32).astype(jnp.bfloat16)
    outgoing = jnp.repeat(outgoing.reshape(experts, capacity, model_width), span, axis=0)
    gate_full, up_full, down_full = weights
    worker = partial(expert_rows, gate_full=gate_full, up_full=up_full, down_full=down_full)
    returned = worker(lax.all_to_all(outgoing, "expert", split_axis=0, concat_axis=0, tiled=True))
    summed = jnp.sum(
        returned.reshape(experts, span, capacity, model_width).astype(jnp.float32), axis=1
    )
    expert_out = summed.astype(jnp.bfloat16).reshape(experts * capacity, model_width)
    picked = jnp.take(expert_out, target, axis=0)
    picked = picked.reshape(tok_rows, fan_out, model_width)
    mixed_sum = jnp.sum(mixing[:, :, None] * picked.astype(jnp.float32), axis=1)
    return (widened + mixed_sum).astype(jnp.bfloat16)


def on_device(blocks, gains, w_gate, w_up, w_down, expert_ids, combine):
    stream = blocks[0]
    turns = expert_ids.shape[1]
    weights = None
    for layer_turn in range(turns):
        if layer_turn > 0:
            stream = passed_along(stream, "section", 1)
        weights = (
            lax.all_gather(w_gate[0], "dp", axis=0, tiled=True),
            lax.all_gather(w_up[0], "dp", axis=0, tiled=True),
            lax.all_gather(w_down[0], "dp", axis=0, tiled=True),
        )
        stream = moe_layer(
            stream, gains[0], weights, expert_ids[0, layer_turn], combine[0, layer_turn]
        )
    return stream[None]


def solution(mesh):
    in_specs = (
        P("section", ("expert", "dp"), None),
        P("section", None),
        P("section", "dp", "expert"),
        P("section", "dp", "expert"),
        P("section", "dp", "expert"),
        P("section", None, ("expert", "dp"), None),
        P("section", None, ("expert", "dp"), None),
    )
    out_specs = P("section", ("expert", "dp"), None)
    return jax.shard_map(
        on_device, mesh=mesh, in_specs=in_specs, out_specs=out_specs, check_vma=False
    )
```

profile of v0, /device:TPU:0, one launch (start us, length us, event | category | flops | bytes accessed | tf_op | source)
XLA Modules:
  0.0 280.1 jit_solution(12629230445887742542)
XLA Ops:
  6.5 0.7 all-gather.7.cloned.1.call-update
  7.3 0.7 all-gather.11.cloned.1.call-update
  8.1 0.7 all-gather.9.cloned.1.call-update
  8.9 0.1 fusion.28
  9.4 0.1 fusion.29
  9.8 0.2 fusion.46
  10.0 0.3 fusion.2
  10.4 29.9 %all_to_all.20 = bf16[8,8,7168]{2,1,0:T(8,128)(2,1)S(1)} all-to-all(bf16[8,8,7168]{2,1,0:T(8,128)(2,1)S(1)} %bitcast.84), channel_id=1, replica_groups=mesh['section'=2,'expert'=8,'dp'=2] {'expert'}, dimensions={0} | all-to-all | bytes 1835008 | tf_op jit(solution)/shard_map/all_to_all | solution.py:56
  40.3 22.2 %all-gather.7.cloned.1.call-done = bf16[1,7168,256]{2,1,0:T(8,128)(2,1)} async-done(((bf16[1,3584,256]{2,1,0:T(8,128)(2,1)}), bf16[1,7168,256]{2,1,0:T(8,128)(2,1)}) %all-gather.7.cloned.1.call-update) | async-done | bytes 3670032 | tf_op jit(solution)/shard_map/all_gather | solution.py:75
  62.5 2.7 fusion.12
  65.3 49.7 %all-gather.11.cloned.1.call-done = bf16[1,7168,256]{2,1,0:T(8,128)(2,1)} async-done(((bf16[1,3584,256]{2,1,0:T(8,128)(2,1)}), bf16[1,7168,256]{2,1,0:T(8,128)(2,1)}) %all-gather.11.cloned.1.call-update) | async-done | bytes 3670032 | tf_op jit(solution)/shard_map/all_gather | solution.py:77
  114.9 52.4 %all-gather.9.cloned.1.call-done = bf16[1,7168,256]{2,1,0:T(8,128)(2,1)} async-done(((bf16[1,3584,256]{2,1,0:T(8,128)(2,1)}), bf16[1,7168,256]{2,1,0:T(8,128)(2,1)}) %all-gather.9.cloned.1.call-update) | async-done | bytes 3670032 | tf_op jit(solution)/shard_map/all_gather | solution.py:76
  167.3 6.8 %fusion = bf16[8,8,7168]{2,1,0:T(8,128)(2,1)} fusion(bf16[1,7168,256]{2,1,0:T(8,128)(2,1)} %all-gather.11.cloned.1.call-done, bf16[1,7168,256]{2,1,0:T(8,128)(2,1)} %all-gather.9.cloned.1.call-done, bf16[8,8,7168]{2,1,0:T(8,128)(2,1)S(1)} %all_to_all.20, f32[64,256]{1,0:T(8,128)S(1)} %fusion.12), kind=kOutput, calls=%fused_computation.4 | convolution fusion | flops 470319104 | bytes 9240576 | tf_op jit(solution)/shard_map/dot_general | solution.py:20
  174.2 4.6 %all-to-all-start.1 = ((bf16[8,8,7168]{2,1,0:T(8,128)(2,1)}), bf16[8,8,7168]{2,1,0:T(8,128)(2,1)S(1)}, u32[]{:S(2)}, u32[]{:S(2)}) async-start(bf16[8,8,7168]{2,1,0:T(8,128)(2,1)} %fusion), calls=%async_computation.1 | async-start | bytes 1835008 | tf_op jit(solution)/shard_map/all_to_all | solution.py:24
  178.9 23.7 %all-to-all-done.1 = bf16[8,8,7168]{2,1,0:T(8,128)(2,1)S(1)} async-done(((bf16[8,8,7168]{2,1,0:T(8,128)(2,1)}), bf16[8,8,7168]{2,1,0:T(8,128)(2,1)S(1)}, u32[]{:S(2)}, u32[]{:S(2)}) %all-to-all-start.1) | async-done | bytes 917536 | tf_op jit(solution)/shard_map/all_to_all | solution.py:24
  202.6 0.1 bitcast_reduce_fusion.1
  202.7 0.7 gather_fusion
  203.5 0.3 reshape.126
  203.8 0.6 multiply_reduce_fusion.1
  204.4 1.5 collective-permute-start
  206.1 3.2 %collective-permute-done = bf16[8,7168]{1,0:T(8,128)(2,1)S(1)} collective-permute-done((bf16[8,7168]{1,0:T(8,128)(2,1)S(1)}, bf16[8,7168]{1,0:T(8,128)(2,1)S(1)}, u32[]{:S(2)}, u32[]{:S(2)}) %collective-permute-start) | collective-permute-done | bytes 114720 | tf_op jit(solution)/shard_map/ppermute | solution.py:11
  209.3 0.2 fusion.42
  209.5 0.3 fusion.3
  209.8 26.4 %all_to_all.21 = bf16[8,8,7168]{2,1,0:T(8,128)(2,1)S(1)} all-to-all(bf16[8,8,7168]{2,1,0:T(8,128)(2,1)S(1)} %bitcast.85), channel_id=1, replica_groups=mesh['section'=2,'expert'=8,'dp'=2] {'expert'}, dimensions={0} | all-to-all | bytes 1835008 | tf_op jit(solution)/shard_map/all_to_all | solution.py:56
  236.3 0.7 fusion.10
  237.0 6.8 %fusion.1 = bf16[8,8,7168]{2,1,0:T(8,128)(2,1)} fusion(bf16[1,7168,256]{2,1,0:T(8,128)(2,1)} %all-gather.11.cloned.1.call-done, bf16[1,7168,256]{2,1,0:T(8,128)(2,1)} %all-gather.9.cloned.1.call-done, bf16[8,8,7168]{2,1,0:T(8,128)(2,1)S(1)} %all_to_all.21, f32[64,256]{1,0:T(8,128)S(1)} %fusion.10), kind=kOutput, calls=%fused_computation.5 | convolution fusion | flops 470319104 | bytes 9240576 | tf_op jit(solution)/shard_map/dot_general | solution.py:20
  243.8 3.6 %all-to-all-start.3 = ((bf16[8,8,7168]{2,1,0:T(8,128)(2,1)}), bf16[8,8,7168]{2,1,0:T(8,128)(2,1)S(1)}, u32[]{:S(2)}, u32[]{:S(2)}) async-start(bf16[8,8,7168]{2,1,0:T(8,128)(2,1)} %fusion.1), calls=%async_computation.3 | async-start | bytes 1835008 | tf_op jit(solution)/shard_map/all_to_all | solution.py:24
  247.5 23.6 %all-to-all-done.3 = bf16[8,8,7168]{2,1,0:T(8,128)(2,1)S(1)} async-done(((bf16[8,8,7168]{2,1,0:T(8,128)(2,1)}), bf16[8,8,7168]{2,1,0:T(8,128)(2,1)S(1)}, u32[]{:S(2)}, u32[]{:S(2)}) %all-to-all-start.3) | async-done | bytes 917536 | tf_op jit(solution)/shard_map/all_to_all | solution.py:24
  271.2 0.7 gather_fusion.1
  272.0 0.3 reshape.127
  272.3 0.6 multiply_reduce_fusion
  272.9 0.7 fusion.51
  (42 shorter events, 1.6 us)
Async XLA Ops:
  6.5 2.2 copy-start.3
  6.5 3.3 %copy-start.1 = (bf16[1,8,7168]{2,1,0:T(8,128)(2,1)S(1)}, bf16[1,8,7168]{2,1,0:T(8,128)(2,1)}, u32[]{:S(2)}) copy-start(bf16[1,8,7168]{2,1,0:T(8,128)(2,1)} %param.9) | copy-start | bytes 344068
  6.5 3.5 %copy-start.2 = (f32[1,7168]{1,0:T(1,128)S(1)}, f32[1,7168]{1,0:T(1,128)}, u32[]{:S(2)}) copy-start(f32[1,7168]{1,0:T(1,128)} %param.10) | copy-start | bytes 86020
  6.5 56.0 %all-gather.7.cloned.1.call-start = ((), (), s32[]{:S(2)}) async-start(), calls=%async_computation.4 | async-start | bytes 5505024 | tf_op jit(solution)/shard_map/all_gather | solution.py:75
  7.3 107.6 %all-gather.11.cloned.1.call-start = ((), (), s32[]{:S(2)}) async-start(), calls=%async_computation.6 | async-start | bytes 5505024 | tf_op jit(solution)/shard_map/all_gather | solution.py:77
  8.0 159.3 %all-gather.9.cloned.1.call-start = ((), (), s32[]{:S(2)}) async-start(), calls=%async_computation.5 | async-start | bytes 5505024 | tf_op jit(solution)/shard_map/all_gather | solution.py:76
  65.2 113.5 %copy-start.4 = (f32[1,2,8,2]{2,3,1,0:T(2,128)S(1)}, f32[1,2,8,2]{2,3,1,0:T(2,128)}, u32[]{:S(2)}) copy-start(f32[1,2,8,2]{2,3,1,0:T(2,128)} %param.15) | copy-start | bytes 388
  174.2 28.4 %all-to-all-start.1 = ((bf16[8,8,7168]{2,1,0:T(8,128)(2,1)}), bf16[8,8,7168]{2,1,0:T(8,128)(2,1)S(1)}, u32[]{:S(2)}, u32[]{:S(2)}) async-start(bf16[8,8,7168]{2,1,0:T(8,128)(2,1)} %fusion), calls=%async_computation.1 | async-start | bytes 1835008 | tf_op jit(solution)/shard_map/all_to_all | solution.py:24
  203.8 32.5 %copy-start = (bf16[1,7168,256]{2,1,0:T(8,128)(2,1)S(1)}, bf16[1,7168,256]{2,1,0:T(8,128)(2,1)}, u32[]{:S(2)}) copy-start(bf16[1,7168,256]{2,1,0:T(8,128)(2,1)} %all-gather.7.cloned.1.call-done) | copy-start | bytes 11010052
  204.4 4.9 %collective-permute-start = (bf16[8,7168]{1,0:T(8,128)(2,1)S(1)}, bf16[8,7168]{1,0:T(8,128)(2,1)S(1)}, u32[]{:S(2)}, u32[]{:S(2)}) collective-permute-start(bf16[8,7168]{1,0:T(8,128)(2,1)S(1)} %fusion.49), channel_id=1, source_target_pairs={{0,16},{16,0},{1,17},{17,1},{2,18},{18,2},{3,19},{19,3},{4,20},{20... | collective-permute-start | bytes 344072 | tf_op jit(solution)/shard_map/ppermute | solution.py:11
  243.8 27.3 %all-to-all-start.3 = ((bf16[8,8,7168]{2,1,0:T(8,128)(2,1)}), bf16[8,8,7168]{2,1,0:T(8,128)(2,1)S(1)}, u32[]{:S(2)}, u32[]{:S(2)}) async-start(bf16[8,8,7168]{2,1,0:T(8,128)(2,1)} %fusion.1), calls=%async_computation.3 | async-start | bytes 1835008 | tf_op jit(solution)/shard_map/all_to_all | solution.py:24
Sparse Core Ops, SparseCore 0:
  8.9 53.5 all-gather.6
  64.0 50.8 all-gather.10
  116.5 50.8 all-gather.8
where the time goes:
time: 280 us
  waiting for transfers between devices  177 us (63%)
  blocking collectives  56.4 us (20%)
  matrix products  18 us (6%)
  between operations  13.3 us (5%)
  starting transfers between devices  9.77 us (3%)
  other arithmetic  3.02 us (1%)
  local copies, waits for them, and re-layouts  2.88 us (1%)
    all_to_all x2, blocking collectives, moe_layer(): lax.all_to_all(outgoing, 'expert', split_axis=0, concat_axis=0, tiled=True)  56.4 us
    all_gather x1, waiting for transfers between devices, on_device(): lax.all_gather(w_up[0], 'dp', axis=0, tiled=True)  52.4 us
    all_gather x1, waiting for transfers between devices, on_device(): lax.all_gather(w_down[0], 'dp', axis=0, tiled=True)  49.7 us
    all_to_all x2, waiting for transfers between devices, expert_rows(): lax.all_to_all(output, 'expert', split_axis=0, concat_axis=0, tiled=True)  47.3 us
    all_gather x1, waiting for transfers between devices, on_device(): lax.all_gather(w_gate[0], 'dp', axis=0, tiled=True)  22.2 us
    dot_general x2, matrix products, expert_rows(): lax.dot_general(hidden, down_full, (((1,), (1,)), ((), ())), preferred_el...  13.6 us
    all_to_all x2, starting transfers between devices, expert_rows(): lax.all_to_all(output, 'expert', split_axis=0, concat_axis=0, tiled=True)  8.16 us
  transfers between devices with their start and end apart: 6, of which 6 were waited for; matrix products, arithmetic and copies ran while one was open for 2% of the time, Pallas kernels for 0%

commit v1 on v0

v1 whole, which is shorter than its diff:
```python
from functools import partial

import jax
import jax.numpy as jnp
from jax import lax
from jax.experimental import pallas as pl
from jax.experimental.pallas import tpu as pltpu
from jax.sharding import PartitionSpec as P

F32 = jnp.float32
BF16 = jnp.bfloat16
MESH = pl.DeviceIdType.MESH


def folded(rows):
    half = rows.shape[1] // 2
    return jnp.concatenate([rows[:, :half], rows[:, half:]], axis=0).astype(BF16)


def unfolded(rows):
    wide = rows.astype(F32)
    count = rows.shape[0] // 2
    return jnp.concatenate([wide[:count], wide[count:]], axis=1)


def kernel(
    owners, sections, turns,
    x_ref, gain_ref, gate_hbm, up_hbm, down_hbm, ids_ref, mix_ref,
    out_ref,
    gate_w, up_w, down_w,
    coef, coef_in, half_out, half_in, rows_all, act_out, act_in,
    part, part_in, chip, chip_in, mixed_out, mixed_in, hop_out, hop_in,
    w_sem, ssem, rsem,
):
    experts = max(2, owners // 8)
    span = owners // experts
    pairs = owners // 2
    sec = lax.axis_index("section")
    own = lax.axis_index("expert")
    p = lax.axis_index("dp")
    z = own // 2
    c = lax.rem(own, 2)
    half = gate_w.shape[0]
    tok = x_ref.shape[1]

    def z_of(d):
        return lax.rem(z + d, pairs)

    sibling = {"expert": 2 * z + 1 - c}
    partner = {"dp": 1 - p}
    onward = {"section": lax.rem(sec + 1, sections)}
    backward = {"section": lax.rem(sec + sections - 1, sections)}

    def peer(d):
        return {"expert": 2 * z_of(d) + c}

    barrier = pltpu.get_barrier_semaphore()
    greeted = [sibling, partner, onward] + [peer(d) for d in range(1, pairs)]
    if sections > 2:
        greeted.append(backward)
    for who in greeted:
        pl.semaphore_signal(barrier, inc=1, device_id=who, device_id_type=MESH)

    loads = [
        pltpu.make_async_copy(src, dst, w_sem.at[i])
        for i, (src, dst) in enumerate(((gate_hbm.at[0], gate_w), (up_hbm.at[0], up_w), (down_hbm.at[0], down_w)))
    ]
    for load in loads:
        load.start()

    counter = [0]

    def send(src, dst, who):
        i = counter[0]
        counter[0] += 1
        copy = pltpu.make_async_remote_copy(
            src_ref=src, dst_ref=dst, send_sem=ssem.at[i], recv_sem=rsem.at[i],
            device_id=who, device_id_type=MESH,
        )
        copy.start()
        return copy

    first = p == 0
    lane = lax.broadcasted_iota(jnp.int32, (tok, 128), 1)
    for r in range(turns):
        ids = ids_ref[0, r]
        mix = mix_ref[0, r]
        table = jnp.zeros((tok, 128), F32)
        for k in range(ids.shape[1]):
            table += jnp.where(lane == ids[:, k : k + 1], mix[:, k : k + 1], 0.0)
        coef[r] = table

    lane16 = lax.broadcasted_iota(jnp.int32, (2 * tok, 128), 1)
    waiting = []
    gain = gain_ref[...]
    stream = x_ref[0].astype(F32)
    for r in range(turns):
        inv = lax.rsqrt(jnp.mean(stream * stream, axis=1, keepdims=True) + 1e-06)
        normed = stream * inv * gain
        lo, hi = normed[:, :half], normed[:, half:]
        keep = jnp.where(first, lo, hi)
        half_out[r] = folded(jnp.where(first, hi, lo))
        if r == 0:
            pl.semaphore_wait(barrier, len(greeted))
            coef_copy = send(coef, coef_in, partner)
            waiting.append(coef_copy)
        copy = send(half_out.at[r], half_in.at[r], partner)
        copy.wait_recv()
        waiting.append(copy)
        other = unfolded(half_in[r])
        block = jnp.concatenate([jnp.where(first, keep, other), jnp.where(first, other, keep)], axis=0)
        rows_all[r, c, z] = block.astype(BF16)

        mine = rows_all.at[r, c, z]
        around = [send(mine, mine, peer(d)) for d in range(1, pairs)]
        across = [send(mine, mine, sibling)]
        for d in range(1, pairs):
            around[d - 1].wait_recv()
            came = rows_all.at[r, c, z_of(pairs - d)]
            across.append(send(came, came, sibling))
        for copy in across:
            copy.wait_recv()
        waiting += around + across

        if r == 0:
            loads[0].wait()
            loads[1].wait()
        rows = rows_all[r].reshape(owners * 2 * tok, half)
        gate = jnp.dot(rows, gate_w[...], preferred_element_type=F32)
        up = jnp.dot(rows, up_w[...], preferred_element_type=F32)
        act_out[r, 0] = gate.astype(BF16)
        act_out[r, 1] = up.astype(BF16)
        copy = send(act_out.at[r], act_in.at[r], partner)
        copy.wait_recv()
        waiting.append(copy)
        gate += act_in[r, 0].astype(F32)
        up += act_in[r, 1].astype(F32)
        hidden = (gate / (1.0 + jnp.exp(-gate)) * up).astype(BF16)

        if r == 0:
            loads[2].wait()
        partial_out = lax.dot_general(
            hidden, down_w[...], (((1,), (1,)), ((), ())), preferred_element_type=F32
        )
        part[r] = partial_out.astype(BF16).reshape(2, pairs, 2 * tok, half)
        copy = send(part.at[r, 1 - c], part_in.at[r], sibling)
        copy.wait_recv()
        waiting.append(copy)

        around = []
        for d in range(1, pairs):
            there = z_of(d)
            chip[r, d] = (part[r, c, there].astype(F32) + part_in[r, there].astype(F32)).astype(BF16)
            around.append(send(chip.at[r, d], chip_in.at[r, d], peer(d)))
        waiting += around

        if r == 0:
            coef_copy.wait_recv()
        mine, theirs = coef[r], coef_in[r]
        table = jnp.concatenate([jnp.where(first, mine, theirs), jnp.where(first, theirs, mine)], axis=0)

        def weight(source):
            return jnp.sum(jnp.where(lane16 == source * 2 // span, table, 0.0), axis=1, keepdims=True)

        total = weight(z) * (part[r, c, z].astype(F32) + part_in[r, z].astype(F32))
        for d in range(1, pairs):
            around[d - 1].wait_recv()
            total += weight(z_of(pairs - d)) * chip_in[r, d].astype(F32)
        keep = jnp.where(first, total[:tok], total[tok:])
        mixed_out[r] = folded(jnp.where(first, total[tok:], total[:tok]))
        copy = send(mixed_out.at[r], mixed_in.at[r], partner)
        copy.wait_recv()
        waiting.append(copy)
        other = unfolded(mixed_in[r])
        stream = stream + jnp.concatenate(
            [jnp.where(first, keep, other), jnp.where(first, other, keep)], axis=1
        )
        if r < turns - 1:
            hop_out[r] = folded(stream)
            copy = send(hop_out.at[r], hop_in.at[r], onward)
            copy.wait_recv()
            waiting.append(copy)
            stream = unfolded(hop_in[r])
        else:
            out_ref[0] = stream.astype(BF16)
    for copy in waiting:
        copy.wait_send()


def on_device(blocks, gains, w_gate, w_up, w_down, expert_ids, combine):
    owners = lax.axis_size("expert")
    sections = lax.axis_size("section")
    turns = expert_ids.shape[1]
    tok = blocks.shape[1]
    width = blocks.shape[2]
    half, cols = w_gate.shape[1:]
    pairs = owners // 2
    rows = 2 * tok
    sends = 1 + turns * (1 + (pairs - 1) + pairs + 1 + 1 + (pairs - 1) + 1) + turns - 1
    vmem = pl.BlockSpec(memory_space=pltpu.VMEM)
    hbm = pl.BlockSpec(memory_space=pl.ANY)
    return pl.pallas_call(
        partial(kernel, owners, sections, turns),
        out_shape=jax.ShapeDtypeStruct(blocks.shape, BF16),
        in_specs=[vmem, vmem, hbm, hbm, hbm, vmem, vmem],
        out_specs=vmem,
        scratch_shapes=[
            pltpu.VMEM((half, cols), BF16),
            pltpu.VMEM((half, cols), BF16),
            pltpu.VMEM((half, cols), BF16),
            pltpu.VMEM((turns, tok, 128), F32),
            pltpu.VMEM((turns, tok, 128), F32),
            pltpu.VMEM((turns, rows, half // 2), BF16),
            pltpu.VMEM((turns, rows, half // 2), BF16),
            pltpu.VMEM((turns, 2, pairs, rows, half), BF16),
            pltpu.VMEM((turns, 2, owners * rows, cols), BF16),
            pltpu.VMEM((turns, 2, owners * rows, cols), BF16),
            pltpu.VMEM((turns, 2, pairs, rows, half), BF16),
            pltpu.VMEM((turns, pairs, rows, half), BF16),
            pltpu.VMEM((turns, pairs, rows, half), BF16),
            pltpu.VMEM((turns, pairs, rows, half), BF16),
            pltpu.VMEM((turns, rows, half // 2), BF16),
            pltpu.VMEM((turns, rows, half // 2), BF16),
            pltpu.VMEM((max(1, turns - 1), rows, width // 2), BF16),
            pltpu.VMEM((max(1, turns - 1), rows, width // 2), BF16),
            pltpu.SemaphoreType.DMA((3,)),
            pltpu.SemaphoreType.DMA((sends,)),
            pltpu.SemaphoreType.DMA((sends,)),
        ],
        compiler_params=pltpu.CompilerParams(
            collective_id=0, has_side_effects=True, vmem_limit_bytes=56 * 2**20
        ),
    )(blocks, gains, w_gate, w_up, w_down, expert_ids, combine)


def solution(mesh):
    in_specs = (
        P("section", ("expert", "dp"), None),
        P("section", None),
        P("section", "dp", "expert"),
        P("section", "dp", "expert"),
        P("section", "dp", "expert"),
        P("section", None, ("expert", "dp"), None),
        P("section", None, ("expert", "dp"), None),
    )
    out_specs = P("section", ("expert", "dp"), None)
    return jax.shard_map(
        on_device, mesh=mesh, in_specs=in_specs, out_specs=out_specs, check_vma=False
    )
```

time: 280 us -> 84 us (0.30)
  waiting for transfers between devices: 177 us -> 0 us
  Pallas kernels: 0 us -> 79.5 us
  blocking collectives: 56.4 us -> 0 us
  matrix products: 18 us -> 0 us
  between operations: 13.3 us -> 0.01 us
  starting transfers between devices: 9.77 us -> 0 us
  other arithmetic: 3.02 us -> 0 us
    all_gather x3 -> x0, waiting for transfers between devices: 124 us -> none  [the longest x1 52.4 us: on_device(): lax.all_gather(w_up[0], 'dp', axis=0, tiled=True)]
    pallas_call x0 -> x1, Pallas kernels: none -> 79.5 us  [on_device(): pl.pallas_call(partial(kernel, owners, sections, turns), out_shape=jax.Sh...]
    all_to_all x2 -> x0, blocking collectives: 56.4 us -> none  [moe_layer(): lax.all_to_all(outgoing, 'expert', split_axis=0, concat_axis=0, tiled=True)]
    all_to_all x2 -> x0, waiting for transfers between devices: 47.3 us -> none  [expert_rows(): lax.all_to_all(output, 'expert', split_axis=0, concat_axis=0, tiled=True)]
    dot_general x8 -> x0, matrix products: 18 us -> none  [the longest x2 13.6 us: expert_rows(): lax.dot_general(hidden, down_full, (((1,), (1,)), ((), ())), preferred_el...]
    all_to_all x2 -> x0, starting transfers between devices: 8.16 us -> none  [expert_rows(): lax.all_to_all(output, 'expert', split_axis=0, concat_axis=0, tiled=True)]
    unnamed x10 -> x3, local copies, waits for them, and re-layouts: 0.02 us -> 4.27 us
    ppermute x1 -> x0, waiting for transfers between devices: 3.24 us -> none  [passed_along(): lax.ppermute(array, axis, [(i, (i + by) % length) for i in range(length)])]
  transfers between devices with their start and end apart: 6 -> 0, of which waited for: 6 -> 0; matrix products, arithmetic and copies ran while one was open for 2% -> 0% of each run, Pallas kernels for 0% -> 0%
where the time goes in v1:
time: 84 us; the launch traced here: 83.8 us
  Pallas kernels  79.5 us (95%)
  local copies, waits for them, and re-layouts  4.27 us (5%)
    pallas_call x1, Pallas kernels, on_device(): pl.pallas_call(partial(kernel, owners, sections, turns), out_shape=jax.Sh...  79.5 us
    unnamed x3, local copies, waits for them, and re-layouts  4.27 us

profile of v1, /device:TPU:0, one launch (start us, length us, event | category | flops | bytes accessed | tf_op | source)
XLA Modules:
  0.0 83.8 jit_solution(2192750299725902058)
XLA Ops:
  0.0 1.4 %copy.8.ids_ref = s32[1,2,8,2]{3,2,1,0:T(8,128)} copy(s32[1,2,8,2]{2,3,1,0:T(2,128)} %param.12) | data formatting | bytes 256 | tf_op args[5]
  1.4 1.4 %copy.9.mix_ref = f32[1,2,8,2]{3,2,1,0:T(8,128)} copy(f32[1,2,8,2]{2,3,1,0:T(2,128)} %param.13) | data formatting | bytes 256 | tf_op args[6]
  2.7 79.5 %shard_map.73 = bf16[1,8,7168]{2,1,0:T(8,128)(2,1)} custom-call(bf16[1,8,7168]{2,1,0:T(8,128)(2,1)} %x_ref.1, f32[1,7168]{1,0:T(1,128)} %gain_ref.1, bf16[1,3584,256]{2,1,0:T(8,128)(2,1)} %gate_hbm.1, bf16[1,3584,256]{2,1,0:T(8,128)(2,1)} %up_hbm.1, bf16[1,3584,256]{2,1,0:T(8,128)(2,1)} %down_hbm.1, s32[1,2,8,2]{3,2,1,0:T(8,128)} %copy.8.ids_ref, ...), custom_call_target="tpu_custom_call" | custom-call | tf_op jit(solution)/shard_map/pallas_call | solution.py:202
  82.3 1.6 %copy.11 = bf16[1,8,7168]{2,1,0:T(8,128)(2,1)} copy(bf16[1,8,7168]{2,1,0:T(8,128)(2,1)} %shard_map.73) | data formatting | bytes 229376

commit v2 on v1

v2 whole, which is shorter than its diff:
```python
from functools import partial

import jax
import jax.numpy as jnp
from jax import lax
from jax.experimental import pallas as pl
from jax.experimental.pallas import tpu as pltpu
from jax.sharding import PartitionSpec as P

F32 = jnp.float32
BF16 = jnp.bfloat16
MESH = pl.DeviceIdType.MESH


def folded(rows):
    half = rows.shape[1] // 2
    return jnp.concatenate([rows[:, :half], rows[:, half:]], axis=0).astype(BF16)


def unfolded(rows):
    wide = rows.astype(F32)
    count = rows.shape[0] // 2
    return jnp.concatenate([wide[:count], wide[count:]], axis=1)


def kernel(
    owners, sections, turns,
    x_ref, gain_ref, gate_hbm, up_hbm, down_hbm, ids_ref, mix_ref,
    out_ref,
    gate_w, up_w, down_w,
    coef, coef_in, half_out, half_in, rows_all, act_out, act_in,
    part, part_in, chip, chip_in, hop_out, hop_in, square_out, square_in, last_out, last_in,
    w_sem, line_s, line_r, pair_s, pair_r, act_s, act_r, part_s, part_r, back_s, back_r, ssem, rsem,
):
    experts = max(2, owners // 8)
    span = owners // experts
    pairs = owners // 2
    sec = lax.axis_index("section")
    own = lax.axis_index("expert")
    p = lax.axis_index("dp")
    z = own // 2
    c = lax.rem(own, 2)
    half = gate_w.shape[0]
    tok = x_ref.shape[1]
    width = x_ref.shape[2]
    ahead, behind = lax.rem(sec + 1, sections), lax.rem(sec + sections - 1, sections)

    sibling = {"expert": 2 * z + 1 - c}
    partner = {"dp": 1 - p}
    onward = {"section": ahead}
    slanted = {"section": ahead, "dp": 1 - p}

    def peer(at):
        return {"expert": 2 * at + c}

    barrier = pltpu.get_barrier_semaphore()
    greeted = [sibling, partner, onward, slanted]
    greeted += [peer(lax.rem(z + d, pairs)) for d in range(1, pairs)]
    if sections > 2:
        greeted += [{"section": behind}, {"section": behind, "dp": 1 - p}]
    for who in greeted:
        pl.semaphore_signal(barrier, inc=1, device_id=who, device_id_type=MESH)

    loads = [
        pltpu.make_async_copy(src, dst, w_sem.at[i])
        for i, (src, dst) in enumerate(((gate_hbm.at[0], gate_w), (up_hbm.at[0], up_w), (down_hbm.at[0], down_w)))
    ]
    for load in loads:
        load.start()

    def remote(src, dst, s, r, who):
        return pltpu.make_async_remote_copy(
            src_ref=src, dst_ref=dst, send_sem=s, recv_sem=r, device_id=who, device_id_type=MESH
        )

    waiting = []
    guarded = []
    counter = [0]

    def start(copy):
        copy.start()
        waiting.append(copy)
        return copy

    def start_if(flag, copy):
        @pl.when(flag)
        def _():
            copy.start()

        guarded.append((flag, copy))

    def send(src, dst, who):
        i = counter[0]
        counter[0] += 1
        return start(remote(src, dst, ssem.at[i], rsem.at[i], who))

    short = jnp.minimum(z, pairs - 1 - z)
    low = 2 * z < pairs - 1
    order = [z]
    for j in range(1, pairs):
        d = (j + 1) // 2
        near = jnp.where(low, -d, d) if j % 2 == 1 else jnp.where(low, d, -d)
        far = jnp.where(low, j - short, short - j)
        order.append(z + jnp.where(j <= 2 * short, near, far))

    first = p == 0
    even = c == 0
    lane = lax.broadcasted_iota(jnp.int32, (tok, 128), 1)
    for r in range(turns):
        ids = ids_ref[0, r]
        mix = mix_ref[0, r]
        table = jnp.zeros((tok, 128), F32)
        for k in range(ids.shape[1]):
            table += jnp.where(lane == ids[:, k : k + 1], mix[:, k : k + 1], 0.0)
        coef[r] = table

    def both(mine, theirs):
        return jnp.concatenate([jnp.where(first, mine, theirs), jnp.where(first, theirs, mine)], axis=0)

    whole = x_ref[0].astype(F32)
    lo, hi = whole[:, :half], whole[:, half:]
    half_out[...] = folded(jnp.where(first, hi, lo))
    squares = jnp.sum(whole * whole, axis=1, keepdims=True)
    coef[turns] = jnp.broadcast_to(squares, (tok, 128))
    pl.semaphore_wait(barrier, len(greeted))
    half_copy = send(half_out, half_in, partner)
    coef_copy = send(coef, coef_in, partner)
    gain = jnp.where(first, gain_ref[:, :half], gain_ref[:, half:])
    half_copy.wait_recv()
    coef_copy.wait_recv()
    stream = both(jnp.where(first, lo, hi), unfolded(half_in[...]))
    squares = both(coef[turns], coef_in[turns])[:, :1]
    lane16 = lax.broadcasted_iota(jnp.int32, (2 * tok, 128), 1)

    for r in range(turns):
        inv = lax.rsqrt(squares / width + 1e-06)
        rows_all[r, z, c] = (stream * inv * gain).astype(BF16)
        mine = rows_all.at[r, z, c]
        left = remote(mine, mine, line_s.at[r, 0], line_r.at[r, z], peer(jnp.maximum(z - 1, 0)))
        right = remote(mine, mine, line_s.at[r, pairs], line_r.at[r, z], peer(jnp.minimum(z + 1, pairs - 1)))
        start_if(z > 0, left)
        start_if(z < pairs - 1, right)
        table = both(coef[r], coef_in[r])

        def weight(source):
            return jnp.sum(jnp.where(lane16 == source * 2 // span, table, 0.0), axis=1, keepdims=True)

        acts, parts, backs, kept = {}, {}, {}, {}

        def multiply(j):
            b = order[j]
            block = rows_all.at[r, b, c]
            if j > 0:
                remote(block, block, line_s.at[r, j], line_r.at[r, b], sibling).wait_recv()
                to = jnp.where(b < z, z + 1, z - 1)
                inside = (to >= 0) & (to < pairs)
                to = jnp.clip(to, 0, pairs - 1)
                start_if(inside, remote(block, block, line_s.at[r, j], line_r.at[r, b], peer(to)))
            start(remote(block, block, pair_s.at[r, j], pair_r.at[r, j], sibling)).wait_recv()
            if r == 0 and j == 0:
                loads[0].wait()
                loads[1].wait()
            rows = rows_all[r, b].reshape(4 * tok, half)
            gate = jnp.dot(rows, gate_w[...], preferred_element_type=F32)
            up = jnp.dot(rows, up_w[...], preferred_element_type=F32)
            act_out[r, j, 0] = gate.astype(BF16)
            act_out[r, j, 1] = up.astype(BF16)
            copy = start(remote(act_out.at[r, j], act_in.at[r, j], act_s.at[r, j], act_r.at[r, j], partner))
            acts[j] = (gate, up, copy)

        def project(j):
            gate, up, copy = acts.pop(j)
            copy.wait_recv()
            gate = gate + act_in[r, j, 0].astype(F32)
            up = up + act_in[r, j, 1].astype(F32)
            hidden = (gate / (1.0 + jnp.exp(-gate)) * up).astype(BF16)
            if r == 0 and j == 0:
                loads[2].wait()
            part[r, j] = lax.dot_general(
                hidden, down_w[...], (((1,), (1,)), ((), ())), preferred_element_type=F32
            ).astype(BF16).reshape(2, 2 * tok, half)
            parts[j] = start(
                remote(part.at[r, j, 1 - c], part_in.at[r, j], part_s.at[r, j], part_r.at[r, j], sibling)
            )

        def give_back(j):
            parts.pop(j).wait_recv()
            summed = part[r, j, c].astype(F32) + part_in[r, j].astype(F32)
            if j == 0:
                kept[0] = weight(z) * summed
            else:
                chip[r, j] = summed.astype(BF16)
                start(remote(chip.at[r, j], chip_in.at[r, z], back_s.at[r, j], back_r.at[r, z], peer(order[j])))

        for j in range(pairs + 2):
            if j < pairs:
                multiply(j)
            if 0 <= j - 1 < pairs:
                project(j - 1)
            if 0 <= j - 2 < pairs:
                give_back(j - 2)

        total = kept[0]
        for j in range(1, pairs):
            b = order[j]
            slot = chip_in.at[r, b]
            remote(slot, slot, back_s.at[r, j], back_r.at[r, b], sibling).wait_recv()
            total += weight(b) * chip_in[r, b].astype(F32)
        after = (stream + total).astype(BF16)
        stream = after.astype(F32)
        if r < turns - 1:
            hop_out[r] = after
            hop = send(hop_out.at[r], hop_in.at[r], onward)
            squares = jnp.sum(stream * stream, axis=1, keepdims=True)
            square_out[r] = jnp.broadcast_to(squares, (2 * tok, 128))
            square = send(square_out.at[r], square_in.at[r], slanted)
            hop.wait_recv()
            stream = hop_in[r].astype(F32)
            squares = jnp.sum(stream * stream, axis=1, keepdims=True)
            square.wait_recv()
            squares += square_in[r][:, :1]
        else:
            keep = jnp.where(first, stream[:tok], stream[tok:])
            last_out[...] = folded(jnp.where(first, stream[tok:], stream[:tok]))
            send(last_out, last_in, partner).wait_recv()
            other = unfolded(last_in[...])
            out_ref[0] = jnp.concatenate(
                [jnp.where(first, keep, other), jnp.where(first, other, keep)], axis=1
            ).astype(BF16)
    for copy in waiting:
        copy.wait_send()
    for flag, copy in guarded:
        pl.when(flag)(copy.wait_send)


def on_device(blocks, gains, w_gate, w_up, w_down, expert_ids, combine):
    owners = lax.axis_size("expert")
    sections = lax.axis_size("section")
    turns = expert_ids.shape[1]
    tok = blocks.shape[1]
    half, cols = w_gate.shape[1:]
    pairs = owners // 2
    rows = 2 * tok
    hops = max(1, turns - 1)
    sends = 3 + 2 * hops
    vmem = pl.BlockSpec(memory_space=pltpu.VMEM)
    hbm = pl.BlockSpec(memory_space=pl.ANY)
    return pl.pallas_call(
        partial(kernel, owners, sections, turns),
        out_shape=jax.ShapeDtypeStruct(blocks.shape, BF16),
        in_specs=[vmem, vmem, hbm, hbm, hbm, vmem, vmem],
        out_specs=vmem,
        scratch_shapes=[
            pltpu.VMEM((half, cols), BF16),
            pltpu.VMEM((half, cols), BF16),
            pltpu.VMEM((half, cols), BF16),
            pltpu.VMEM((turns + 1, tok, 128), F32),
            pltpu.VMEM((turns + 1, tok, 128), F32),
            pltpu.VMEM((rows, half // 2), BF16),
            pltpu.VMEM((rows, half // 2), BF16),
            pltpu.VMEM((turns, pairs, 2, rows, half), BF16),
            pltpu.VMEM((turns, pairs, 2, 2 * rows, cols), BF16),
            pltpu.VMEM((turns, pairs, 2, 2 * rows, cols), BF16),
            pltpu.VMEM((turns, pairs, 2, rows, half), BF16),
            pltpu.VMEM((turns, pairs, rows, half), BF16),
            pltpu.VMEM((turns, pairs, rows, half), BF16),
            pltpu.VMEM((turns, pairs, rows, half), BF16),
            pltpu.VMEM((hops, rows, half), BF16),
            pltpu.VMEM((hops, rows, half), BF16),
            pltpu.VMEM((hops, rows, 128), F32),
            pltpu.VMEM((hops, rows, 128), F32),
            pltpu.VMEM((rows, half // 2), BF16),
            pltpu.VMEM((rows, half // 2), BF16),
            pltpu.SemaphoreType.DMA((3,)),
            pltpu.SemaphoreType.DMA((turns, pairs + 1)),
        ]
        + [pltpu.SemaphoreType.DMA((turns, pairs))] * 9
        + [pltpu.SemaphoreType.DMA((sends,))] * 2,
        compiler_params=pltpu.CompilerParams(
            collective_id=0, has_side_effects=True, vmem_limit_bytes=56 * 2**20
        ),
    )(blocks, gains, w_gate, w_up, w_down, expert_ids, combine)


def solution(mesh):
    in_specs = (
        P("section", ("expert", "dp"), None),
        P("section", None),
        P("section", "dp", "expert"),
        P("section", "dp", "expert"),
        P("section", "dp", "expert"),
        P("section", None, ("expert", "dp"), None),
        P("section", None, ("expert", "dp"), None),
    )
    out_specs = P("section", ("expert", "dp"), None)
    return jax.shard_map(
        on_device, mesh=mesh, in_specs=in_specs, out_specs=out_specs, check_vma=False
    )
```

time: 84 us -> 76.3 us (0.908)
  Pallas kernels: 79.5 us -> 71.8 us
    pallas_call x1, Pallas kernels: 79.5 us -> 71.8 us  [on_device(): pl.pallas_call(partial(kernel, owners, sections, turns), out_shape=jax.Sh...]
where the time goes in v2:
time: 76.3 us; the launch traced here: 76.1 us
  Pallas kernels  71.8 us (94%)
  local copies, waits for them, and re-layouts  4.27 us (6%)
    pallas_call x1, Pallas kernels, on_device(): pl.pallas_call(partial(kernel, owners, sections, turns), out_shape=jax.Sh...  71.8 us
    unnamed x3, local copies, waits for them, and re-layouts  4.27 us

profile of v2, /device:TPU:0, one launch (start us, length us, event | category | flops | bytes accessed | tf_op | source)
XLA Modules:
  0.0 76.1 jit_solution(2419856105607248544)
XLA Ops:
  0.0 1.4 %copy.8.ids_ref = s32[1,2,8,2]{3,2,1,0:T(8,128)} copy(s32[1,2,8,2]{2,3,1,0:T(2,128)} %param.12) | data formatting | bytes 256 | tf_op args[5]
  1.4 1.4 %copy.9.mix_ref = f32[1,2,8,2]{3,2,1,0:T(8,128)} copy(f32[1,2,8,2]{2,3,1,0:T(2,128)} %param.13) | data formatting | bytes 256 | tf_op args[6]
  2.7 71.8 %shard_map.73 = bf16[1,8,7168]{2,1,0:T(8,128)(2,1)} custom-call(bf16[1,8,7168]{2,1,0:T(8,128)(2,1)} %x_ref.1, f32[1,7168]{1,0:T(1,128)} %gain_ref.1, bf16[1,3584,256]{2,1,0:T(8,128)(2,1)} %gate_hbm.1, bf16[1,3584,256]{2,1,0:T(8,128)(2,1)} %up_hbm.1, bf16[1,3584,256]{2,1,0:T(8,128)(2,1)} %down_hbm.1, s32[1,2,8,2]{3,2,1,0:T(8,128)} %copy.8.ids_ref, ...), custom_call_target="tpu_custom_call" | custom-call | tf_op jit(solution)/shard_map/pallas_call | solution.py:248
  74.5 1.6 %copy.11 = bf16[1,8,7168]{2,1,0:T(8,128)(2,1)} copy(bf16[1,8,7168]{2,1,0:T(8,128)(2,1)} %shard_map.73) | data formatting | bytes 229376
